TPU v7x, 32 devices: a whole 2x2x4 slice. The times are simulated.
32 devices in a mesh: blk: 8 (over z, y), trk: 4 (over x, core).
Axes of the slice: x: 2, y: 2, z: 4, core: 2. Of those that a mesh axis runs over, the one named last changes fastest.
Arguments:
- row_block: int32 [8192, 1], P(('blk', 'trk')), may hold values from 0 to 7; in each aligned block of 256 rows (0 to 255, 256 to 511, ...) at most 64 rows name the same one
- row_hits: int32 [2, 8192], P(None, ('blk', 'trk')), may hold values from 0 to 63
- row_slot: int32 [8192], P(('blk', 'trk')), may hold values from 0 to 4
- track_kept: int32 [1024], P(('blk', 'trk')), may hold values 0 or 1
- row_derivs: bfloat16 [12, 8192], P(None, ('blk', 'trk')), may hold values from -0.75 to 0.75
- row_resid: bfloat16 [8192], P(('blk', 'trk')), may hold values from -6 to 6
- row_invsig: bfloat16 [8192], P(('blk', 'trk')), may hold values from 0.5 to 2
- pattern: int32 [8, 5], P('blk'), may hold values from 0 to 7, as said below
- prior: float32 [8, 384], P('blk'), may hold values from 0.2 to 3
Outputs:
- solution: float32 [8, 384], P('blk')
- gradient: float32 [8, 384], P('blk')
Inputs may be any that keep to these rules, and one draw needn't show every extreme that they name: `row_block`: among the rows of one device (aligned blocks of 256 rows) no block is named by more than 64 rows, and in every draw some device's rows name some block exactly 64 times. `pattern`: row k lists the blocks k - 2, k - 1, k, k + 1, k + 2 modulo 8, each once, in an order of its own.
All inputs are finite; a program needn't handle non-finite values. No bound on the sum of `track_kept` on one device may be relied on, other than what follows from the above.
Results may differ from a plain program's by a relative error of at most 0.0036.
The roundings to bfloat16 on the way count: a program that leaves them out, or rounds other values in their place, can miss the bound.
Values may be sent and summed in bfloat16 or wider, within the bound.
A program may use at most 64 MiB of HBM per device.

v0:
```python
import functools

import jax
import jax.numpy as jnp
from jax import lax
from jax.experimental import pallas as pl
from jax.experimental.pallas import tpu as pltpu
from jax.sharding import PartitionSpec as P

MODS = 64
PAR = 6
NB = 5
SEG = 8
ITERS = 2


epsilon = 1e-06


def passed_along(block, axis, distance):
    devices = range(lax.axis_size(axis))
    route = [((i - distance) % len(devices), i) for i in devices]
    return lax.ppermute(block, axis, route)


def project(initial_norm, diag_terms, off_terms, basis_list):
    size_count = len(diag_terms)
    zero_value = diag_terms[0] * 0.0
    rows_list = []
    for row_index in range(size_count + 1):
        entries = []
        for column in range(size_count):
            if row_index == column:
                entries.append(diag_terms[column])
            elif row_index == column + 1:
                entries.append(off_terms[column])
            elif column == row_index + 1:
                entries.append(off_terms[row_index])
            else:
                entries.append(zero_value)
        rows_list.append(jnp.stack(entries))
    tridiagonal = jnp.stack(rows_list)
    gram_matrix = jnp.dot(tridiagonal.T, tridiagonal, precision=lax.Precision.HIGHEST)
    target = initial_norm * tridiagonal[0]
    factor = jnp.linalg.cholesky(gram_matrix)
    forward = []
    for row_index in range(size_count):
        partial_sum = target[row_index]
        for column in range(row_index):
            partial_sum = partial_sum - factor[row_index, column] * forward[column]
        forward.append(partial_sum / factor[row_index, row_index])
    backward = [zero_value] * size_count
    for row_index in reversed(range(size_count)):
        partial_sum = forward[row_index]
        for column in range(row_index + 1, size_count):
            partial_sum = partial_sum - factor[column, row_index] * backward[column]
        backward[row_index] = partial_sum / factor[row_index, row_index]
    solution = backward[0] * basis_list[0]
    row_index = 1
    solution = solution + backward[row_index] * basis_list[row_index]
    return solution


def contract(left_rows, right_rows):
    return lax.dot_general(
        left_rows, right_rows, (((0,), (0,)), ((), ())), preferred_element_type=jnp.float32
    )


def on_device_large(
    row_block, row_hits, row_slot, track_kept, row_derivs, row_resid, row_invsig, pattern, prior
):
    row_count = row_resid.shape[0]
    owners = lax.axis_size("blk")
    capacity = 2 * row_count // owners
    order_size = MODS * PAR
    kept_rows = jnp.repeat(track_kept, SEG).astype(jnp.float32)
    scaling = kept_rows * row_invsig.astype(jnp.float32)
    scaled = (scaling[None, :] * row_derivs.astype(jnp.float32)).astype(jnp.bfloat16)
    weighted = (scaling * row_resid.astype(jnp.float32)).astype(jnp.bfloat16)
    destination = row_block[:, 0]
    member = (destination[:, None] == jnp.arange(owners, dtype=jnp.int32)[None, :]).astype(
        jnp.bfloat16
    )
    row_ids = jnp.arange(row_count, dtype=jnp.int32)
    earlier = (row_ids[:, None] > row_ids[None, :]).astype(jnp.bfloat16)
    before = jnp.dot(earlier, member, preferred_element_type=jnp.float32)
    rank_within = jnp.sum(before * member.astype(jnp.float32), axis=1).astype(jnp.int32)
    slot_place = destination * capacity + rank_within
    labels = jnp.stack([row_hits[0], row_hits[1], row_slot]).astype(jnp.bfloat16)
    record = jnp.concatenate([scaled, weighted[None, :], labels], axis=0)
    outgoing = (
        jnp.zeros((record.shape[0], owners * capacity), jnp.bfloat16).at[:, slot_place].set(record)
    )
    incoming = lax.all_to_all(outgoing, "blk", split_axis=1, concat_axis=1, tiled=True)
    column_ids = jnp.arange(order_size, dtype=jnp.int32)
    column_module = column_ids // PAR
    column_param = column_ids % PAR

    def expand(values, module_ids):
        spread = jnp.zeros((values.shape[1], order_size), jnp.bfloat16)
        for component in range(PAR):
            spread = jnp.where(
                column_param[None, :] == component, values[component][:, None], spread
            )
        return jnp.where(
            module_ids[:, None] == column_module[None, :], spread, jnp.zeros_like(spread)
        )

    first_module = incoming[2 * PAR + 1].astype(jnp.int32)
    second_module = incoming[2 * PAR + 2].astype(jnp.int32)
    slot_in = incoming[2 * PAR + 3].astype(jnp.int32)
    resid_in = incoming[2 * PAR]
    first_rows = expand(incoming[0:PAR], first_module)
    second_rows = expand(incoming[PAR : 2 * PAR], second_module)
    own_block = contract(first_rows, first_rows)
    grad_own = jnp.dot(resid_in, first_rows, preferred_element_type=jnp.float32)
    cross_list, partner_list, grad_list = ([], [], [])
    for slot_id in range(NB):
        masked = jnp.where((slot_in == slot_id)[:, None], second_rows, jnp.zeros_like(second_rows))
        cross_list.append(contract(first_rows, masked))
        partner_list.append(contract(masked, masked))
        grad_list.append(jnp.dot(resid_in, masked, preferred_element_type=jnp.float32))
    cross_blocks = jnp.stack(cross_list)
    partner_blocks = jnp.stack(partner_list)
    grad_partner = jnp.stack(grad_list)
    position = lax.axis_index("blk")
    neighbours = pattern[0]
    offset = (neighbours - position) % owners
    offset = jnp.where(offset > owners // 2, offset - owners, offset)

    def deliver(own_term, partner_terms):
        local_sum = own_term + jnp.sum(
            jnp.where((offset == 0)[:, None], partner_terms, 0.0), axis=0, keepdims=True
        )
        for shift_by in (-2, -1, 1, 2):
            sending = jnp.sum(
                jnp.where((offset == shift_by)[:, None], partner_terms, 0.0), axis=0, keepdims=True
            )
            local_sum = local_sum + passed_along(sending, "blk", shift_by)
        return lax.psum(local_sum, "trk")

    gradient = deliver(grad_own[None, :], grad_partner)
    initial_norm = jnp.sqrt(lax.psum(jnp.sum(gradient * gradient), "blk") + epsilon)
    current = gradient / initial_norm
    previous = jnp.zeros_like(gradient)
    beta_term = jnp.zeros((), jnp.float32)
    diag_terms, off_terms, basis_list = ([], [], [])
    for iteration in range(ITERS):
        result = jnp.where((offset == 0)[:, None], current, 0.0)
        for fetch_shift_by in (-2, -1, 1, 2):
            arrived = passed_along(current, "blk", -fetch_shift_by)
            result = result + jnp.where((offset == fetch_shift_by)[:, None], arrived, 0.0)
        operate_own_term = jnp.dot(own_block, current[0], precision=lax.Precision.HIGHEST)
        operate_own_term = operate_own_term + jnp.einsum(
            "kij,kj->i", cross_blocks, result, precision=lax.Precision.HIGHEST
        )
        operate_partner_terms = jnp.einsum(
            "kij,i->kj", cross_blocks, current[0], precision=lax.Precision.HIGHEST
        )
        operate_partner_terms = operate_partner_terms + jnp.einsum(
            "kij,kj->ki", partner_blocks, result, precision=lax.Precision.HIGHEST
        )
        image_vec = prior * current + deliver(operate_own_term[None, :], operate_partner_terms)
        alpha_term = lax.psum(jnp.sum(current * image_vec), "blk")
        direction = image_vec - alpha_term * current - beta_term * previous
        beta_next = jnp.sqrt(lax.psum(jnp.sum(direction * direction), "blk") + epsilon)
        diag_terms.append(alpha_term)
        off_terms.append(beta_next)
        basis_list.append(current)
        previous, current, beta_term = (current, direction / beta_next, beta_next)
    solution = project(initial_norm, diag_terms, off_terms, basis_list)
    return (solution, gradient)


LANES = 128
WIDE = 8
PHASES = ITERS + 1


def two_parts(value):
    high = value.astype(jnp.bfloat16)
    low = (value - high.astype(jnp.float32)).astype(jnp.bfloat16)
    return jnp.concatenate([high, low], axis=0)


def three_parts(value):
    high = value.astype(jnp.bfloat16).astype(jnp.float32)
    rest = value - high
    middle = rest.astype(jnp.bfloat16).astype(jnp.float32)
    return jnp.concatenate([high, middle, rest - middle], axis=0).astype(jnp.bfloat16)


def total(value):
    return jnp.sum(jnp.sum(value, axis=0, keepdims=True), axis=1, keepdims=True)


def kernel(
    owners,
    shares,
    block_ref,
    hits_ref,
    slot_ref,
    kept_ref,
    derivs_ref,
    resid_ref,
    invsig_ref,
    pattern_ref,
    prior_ref,
    out_ref,
    onehot,
    table,
    part,
    landed,
    blocks,
    full,
    table_send,
    table_recv,
    part_send,
    part_recv,
    block_send,
    block_recv,
    full_send,
    full_recv,
):
    blk, trk = lax.axis_index("blk"), lax.axis_index("trk")
    rows = block_ref.shape[1]
    tracks = kept_ref.shape[1]
    modules = owners * MODS
    order_size = MODS * PAR
    per_share = LANES // MODS

    def other_blk(distance):
        return {"blk": lax.rem(blk + distance, owners), "trk": trk}

    def other_trk(distance):
        return {"blk": blk, "trk": lax.rem(trk + distance, shares)}

    peers = [other_blk(d) for d in range(1, owners)] + [other_trk(d) for d in range(1, shares)]
    barrier = pltpu.get_barrier_semaphore()
    for peer in peers:
        pl.semaphore_signal(barrier, inc=1, device_id=peer, device_id_type=pl.DeviceIdType.MESH)

    def copy(source, target, send, recv, peer):
        return pltpu.make_async_remote_copy(
            src_ref=source,
            dst_ref=target,
            send_sem=send,
            recv_sem=recv,
            device_id=peer,
            device_id_type=pl.DeviceIdType.MESH,
        )

    started = []

    table[blk, :, 0:NB] = pattern_ref[...]
    pl.semaphore_wait(barrier, len(peers))
    sent = [
        copy(table.at[blk], table.at[blk], table_send.at[d - 1], table_recv.at[d - 1], other_blk(d))
        for d in range(1, owners)
    ]
    for one in sent:
        one.start()
    started += sent

    track_of = lax.broadcasted_iota(jnp.int32, (tracks, rows), 1) // SEG
    track_id = lax.broadcasted_iota(jnp.int32, (tracks, rows), 0)
    kept_rows = jnp.dot(
        jnp.broadcast_to(kept_ref[...].astype(jnp.float32), (WIDE, tracks)).astype(jnp.bfloat16),
        (track_of == track_id).astype(jnp.float32).astype(jnp.bfloat16),
        preferred_element_type=jnp.float32,
    )[0:1]
    scaling = kept_rows * invsig_ref[...].astype(jnp.float32)
    scaled = (scaling * derivs_ref[...].astype(jnp.float32)).astype(jnp.bfloat16).astype(jnp.float32)
    weighted = (scaling * resid_ref[...].astype(jnp.float32)).astype(jnp.bfloat16).astype(jnp.float32)
    none = jnp.zeros((WIDE - PAR, rows), jnp.float32)
    derivs = jnp.concatenate(
        [
            jnp.concatenate([scaled[0:PAR], none], axis=0),
            jnp.concatenate([scaled[PAR : 2 * PAR], none], axis=0),
        ],
        axis=1,
    )
    first_block = block_ref[...]
    first_module = first_block * MODS + hits_ref[0:1]
    module_ids = lax.broadcasted_iota(jnp.int32, (modules, rows), 0)
    onehot[:, 0:rows] = (module_ids == first_module).astype(jnp.float32).astype(jnp.bfloat16)

    place_row = lax.broadcasted_iota(jnp.int32, (order_size, LANES), 0) // PAR
    place_lane = lax.broadcasted_iota(jnp.int32, (order_size, LANES), 1)
    half = lax.rem(blk, per_share)
    place = (place_lane == place_row + half * MODS).astype(jnp.float32).astype(jnp.bfloat16)
    component = lax.broadcasted_iota(jnp.int32, (WIDE, order_size), 0)
    parameter = lax.broadcasted_iota(jnp.int32, (WIDE, order_size), 1)
    own_entry = component == lax.rem(parameter, PAR)
    spread_prior = jnp.where(own_entry, prior_ref[...], 0.0)
    prior_parts = jnp.dot(three_parts(spread_prior), place, preferred_element_type=jnp.float32)
    own_prior = prior_parts[0:WIDE] + prior_parts[WIDE : 2 * WIDE] + prior_parts[2 * WIDE :]
    own_prior = jnp.where(trk == 0, own_prior, 0.0)
    own_share = blk // per_share
    prior = [jnp.where(own_share == j, own_prior, 0.0) for j in range(shares)]

    def in_order(vector_ref):
        parts = three_parts(vector_ref[own_share])
        laid = lax.dot_general(
            parts, place, (((1,), (1,)), ((), ())), preferred_element_type=jnp.float32
        )
        laid = laid[0:WIDE] + laid[WIDE : 2 * WIDE] + laid[2 * WIDE :]
        return jnp.sum(jnp.where(own_entry, laid, 0.0), axis=0, keepdims=True)

    for one in sent:
        one.wait_recv()
    patterns = table[...].reshape(owners, LANES).astype(jnp.float32)
    block_ids = lax.broadcasted_iota(jnp.int32, (owners, rows), 0)
    names = (block_ids == first_block).astype(jnp.float32)
    slot = slot_ref[...]
    second_block = jnp.zeros((1, rows), jnp.float32)
    for s in range(NB):
        value = jnp.sum(names * patterns[:, s : s + 1], axis=0, keepdims=True)
        second_block = jnp.where(slot == s, value, second_block)
    second_module = second_block.astype(jnp.int32) * MODS + hits_ref[1:2]
    onehot[:, rows : 2 * rows] = (module_ids == second_module).astype(jnp.float32).astype(jnp.bfloat16)

    def scatter(row_values):
        both = jnp.concatenate([row_values, row_values], axis=1)
        summed = lax.dot_general(
            two_parts(derivs * both),
            onehot[...],
            (((1,), (1,)), ((), ())),
            preferred_element_type=jnp.float32,
        )
        return summed[0:WIDE] + summed[WIDE : 2 * WIDE]

    def gather(vector):
        read = jnp.dot(two_parts(vector), onehot[...], preferred_element_type=jnp.float32)
        read = read[0:WIDE] + read[WIDE : 2 * WIDE]
        along = jnp.sum(derivs * read, axis=0, keepdims=True)
        return along[:, 0:rows] + along[:, rows : 2 * rows]

    def add_up(phase, terms):
        for j in range(shares):
            part[phase, j] = terms[j]
        sent = []
        for d in range(1, shares):
            sent.append(
                copy(
                    part.at[phase, lax.rem(trk + d, shares)],
                    landed.at[phase, d - 1],
                    part_send.at[phase, d - 1],
                    part_recv.at[phase, d - 1],
                    other_trk(d),
                )
            )
        for one in sent:
            one.start()
        own = part[phase, trk]
        for one in sent:
            one.wait_recv()
        started.extend(sent)
        for d in range(1, shares):
            own = own + landed[phase, d - 1]
        blocks[phase, blk] = own
        sent = []
        for d in range(1, owners):
            sent.append(
                copy(
                    blocks.at[phase, blk],
                    blocks.at[phase, blk],
                    block_send.at[phase, d - 1],
                    block_recv.at[phase, d - 1],
                    other_blk(d),
                )
            )
        for one in sent:
            one.start()
        for one in sent:
            one.wait_recv()
        started.extend(sent)
        summed = blocks[phase, 0]
        for k in range(1, owners):
            summed = summed + blocks[phase, k]
        full[phase, trk] = summed
        sent = []
        for d in range(1, shares):
            sent.append(
                copy(
                    full.at[phase, trk],
                    full.at[phase, trk],
                    full_send.at[phase, d - 1],
                    full_recv.at[phase, d - 1],
                    other_trk(d),
                )
            )
        for one in sent:
            one.start()
        for one in sent:
            one.wait_recv()
        started.extend(sent)
        return jnp.concatenate([full[phase, j] for j in range(shares)], axis=1)

    def pieces(vector):
        return [vector[:, j * LANES : (j + 1) * LANES] for j in range(shares)]

    gradient = add_up(0, pieces(scatter(weighted)))
    initial_norm = jnp.sqrt(total(gradient * gradient) + epsilon)
    current = gradient / initial_norm
    previous = jnp.zeros_like(gradient)
    beta_term = jnp.zeros((1, 1), jnp.float32)
    diag_terms, off_terms, basis_list = ([], [], [])
    for iteration in range(ITERS):
        terms = pieces(scatter(gather(current)))
        for j, values in enumerate(pieces(current)):
            terms[j] = terms[j] + prior[j] * values
        image_vec = add_up(iteration + 1, terms)
        alpha_term = total(current * image_vec)
        direction = image_vec - alpha_term * current - beta_term * previous
        beta_next = jnp.sqrt(total(direction * direction) + epsilon)
        diag_terms.append(alpha_term)
        off_terms.append(beta_next)
        basis_list.append(current)
        previous, current, beta_term = (current, direction / beta_next, beta_next)
    out_ref[1:2] = in_order(full.at[0])

    first, second = diag_terms
    below, last = off_terms
    corner = first * first + below * below
    side = first * below + below * second
    end = below * below + second * second + last * last
    root = jnp.sqrt(corner)
    lower = side / root
    tip = jnp.sqrt(end - lower * lower)
    forward = initial_norm * first / root
    forward_next = (initial_norm * below - lower * forward) / tip
    back_next = forward_next / tip
    back = (forward - lower * back_next) / root
    result = back * basis_list[0] + back_next * basis_list[1]
    for j, values in enumerate(pieces(result)):
        part[PHASES, j] = values
    out_ref[0:1] = in_order(part.at[PHASES])
    for one in started:
        one.wait_send()


def on_device(
    row_block,
    row_hits,
    row_slot,
    track_kept,
    row_derivs,
    row_resid,
    row_invsig,
    pattern,
    prior,
    owners,
    shares,
):
    args = (
        row_block, row_hits, row_slot, track_kept, row_derivs, row_resid, row_invsig, pattern, prior
    )
    if owners * MODS != shares * LANES:
        return on_device_large(*args)
    rows = row_resid.shape[0]
    dma = pltpu.SemaphoreType.DMA
    tile = (WIDE, LANES)
    out = pl.pallas_call(
        functools.partial(kernel, owners, shares),
        out_shape=jax.ShapeDtypeStruct((2, MODS * PAR), jnp.float32),
        in_specs=[pl.BlockSpec(memory_space=pltpu.VMEM)] * 9,
        out_specs=pl.BlockSpec(memory_space=pltpu.VMEM),
        scratch_shapes=[
            pltpu.VMEM((owners * MODS, 2 * rows), jnp.bfloat16),
            pltpu.VMEM((owners, 1, LANES), jnp.int32),
            pltpu.VMEM((PHASES + 1, shares) + tile, jnp.float32),
            pltpu.VMEM((PHASES, shares - 1) + tile, jnp.float32),
            pltpu.VMEM((PHASES, owners) + tile, jnp.float32),
            pltpu.VMEM((PHASES + 1, shares) + tile, jnp.float32),
            dma((owners - 1,)),
            dma((owners - 1,)),
            dma((PHASES, shares - 1)),
            dma((PHASES, shares - 1)),
            dma((PHASES, owners - 1)),
            dma((PHASES, owners - 1)),
            dma((PHASES, shares - 1)),
            dma((PHASES, shares - 1)),
        ],
        compiler_params=pltpu.CompilerParams(
            collective_id=0, has_side_effects=True, vmem_limit_bytes=16 * 1024 * 1024
        ),
    )(
        row_block.reshape(1, rows),
        row_hits,
        row_slot.reshape(1, rows),
        track_kept.reshape(1, -1),
        row_derivs,
        row_resid.reshape(1, rows),
        row_invsig.reshape(1, rows),
        pattern,
        prior,
    )
    return out[0:1], out[1:2]


def solution(mesh):
    return jax.shard_map(
        functools.partial(on_device, owners=mesh.shape["blk"], shares=mesh.shape["trk"]),
        mesh=mesh,
        in_specs=(
            P(("blk", "trk"), None),
            P(None, ("blk", "trk")),
            P(("blk", "trk")),
            P(("blk", "trk")),
            P(None, ("blk", "trk")),
            P(("blk", "trk")),
            P(("blk", "trk")),
            P("blk", None),
            P("blk", None),
        ),
        out_specs=(P("blk", None), P("blk", None)),
        check_vma=False,
    )
```

profile of v0, /device:TPU:1, one launch (start us, length us, event | category | flops | bytes accessed | tf_op | source)
XLA Modules:
  0.0 45.7 jit_solution(16752349677125506179)
XLA Ops:
  0.6 0.0 copy-start
  0.6 0.7 %reshape.22.resid_ref = bf16[1,256]{1,0:T(2,128)(2,1)S(1)} reshape(bf16[256]{0:T(256)(128)(2,1)} %param.14) | data formatting | bytes 1024 | tf_op jit(solution)/shard_map/reshape | solution.py:495
  1.3 0.0 copy-start.3
  1.3 0.7 %reshape.23.invsig_ref = bf16[1,256]{1,0:T(2,128)(2,1)S(1)} reshape(bf16[256]{0:T(256)(128)(2,1)} %param.15) | data formatting | bytes 1024 | tf_op jit(solution)/shard_map/reshape | solution.py:496
  2.0 0.0 copy-done
  2.0 0.0 copy-done.3
  2.0 0.0 copy-start.1
  2.0 0.7 %copy-done.1 = s32[2,256]{1,0:T(2,128)S(1)} copy-done((s32[2,256]{1,0:T(2,128)S(1)}, s32[2,256]{1,0:T(2,128)}, u32[]{:S(2)}) %copy-start.1) | copy-done | bytes 2072
  2.7 0.0 copy-start.2
  2.7 0.7 %copy-done.2 = f32[1,384]{1,0:T(1,128)S(1)} copy-done((f32[1,384]{1,0:T(1,128)S(1)}, f32[1,384]{1,0:T(1,128)}, u32[]{:S(2)}) %copy-start.2) | copy-done | bytes 1560
  3.3 0.0 copy-start.4
  3.4 0.7 %copy-done.4 = s32[256]{0:T(256)S(1)} copy-done((s32[256]{0:T(256)S(1)}, s32[256]{0:T(256)}, u32[]{:S(2)}) %copy-start.4) | copy-done | bytes 1048
  4.0 0.0 copy-start.5
  4.0 0.7 %copy-done.5 = s32[32]{0:T(128)S(1)} copy-done((s32[32]{0:T(128)S(1)}, s32[32]{0:T(128)}, u32[]{:S(2)}) %copy-start.5) | copy-done | bytes 152
  4.7 0.0 copy-start.6
  4.7 0.7 %copy-done.6 = s32[1,5]{1,0:T(1,128)S(1)} copy-done((s32[1,5]{1,0:T(1,128)S(1)}, s32[1,5]{1,0:T(1,128)}, u32[]{:S(2)}) %copy-start.6) | copy-done | bytes 44
  5.3 39.8 %shard_map.104 = f32[2,384]{1,0:T(2,128)S(1)} custom-call(s32[1,256]{1,0:T(1,128)S(1)} %bitcast.3, s32[2,256]{1,0:T(2,128)S(1)} %copy-done.1, s32[1,256]{1,0:T(1,128)S(1)} %bitcast.4, s32[1,32]{1,0:T(1,128)S(1)} %bitcast.5, bf16[12,256]{1,0:T(8,128)(2,1)S(1)} %copy-done, bf16[1,256]{1,0:T(2,128)(2,1)S(1)} %reshape.22.resid_ref, ...), custom_call_target="tpu_custom_call" | custom-call | tf_op jit(solution)/shard_map/pallas_call | solution.py:465
  45.2 0.6 %fusion = (f32[1,384]{1,0:T(1,128)}, f32[1,384]{1,0:T(1,128)}) fusion(f32[2,384]{1,0:T(2,128)S(1)} %shard_map.104), kind=kLoop, calls=%fused_computation | loop fusion | bytes 6144 | tf_op jit(solution)/shard_map/slice | solution.py:500
Async XLA Ops:
  0.6 1.4 %copy-start = (bf16[12,256]{1,0:T(8,128)(2,1)S(1)}, bf16[12,256]{1,0:T(8,128)(2,1)}, u32[]{:S(2)}) copy-start(bf16[12,256]{1,0:T(8,128)(2,1)} %derivs_ref.1) | copy-start | bytes 18436
  1.3 0.7 %copy-start.3 = (s32[256,1]{0,1:T(1,128)S(1)}, s32[256,1]{0,1:T(1,128)}, u32[]{:S(2)}) copy-start(s32[256,1]{0,1:T(1,128)} %param.9) | copy-start | bytes 3076
  2.0 0.7 %copy-start.1 = (s32[2,256]{1,0:T(2,128)S(1)}, s32[2,256]{1,0:T(2,128)}, u32[]{:S(2)}) copy-start(s32[2,256]{1,0:T(2,128)} %hits_ref.1) | copy-start | bytes 6148
  2.7 0.7 %copy-start.2 = (f32[1,384]{1,0:T(1,128)S(1)}, f32[1,384]{1,0:T(1,128)}, u32[]{:S(2)}) copy-start(f32[1,384]{1,0:T(1,128)} %prior_ref.1) | copy-start | bytes 4612
  3.3 0.7 %copy-start.4 = (s32[256]{0:T(256)S(1)}, s32[256]{0:T(256)}, u32[]{:S(2)}) copy-start(s32[256]{0:T(256)} %param.11) | copy-start | bytes 3076
  4.0 0.7 %copy-start.5 = (s32[32]{0:T(128)S(1)}, s32[32]{0:T(128)}, u32[]{:S(2)}) copy-start(s32[32]{0:T(128)} %param.12) | copy-start | bytes 388
  4.7 0.7 %copy-start.6 = (s32[1,5]{1,0:T(1,128)S(1)}, s32[1,5]{1,0:T(1,128)}, u32[]{:S(2)}) copy-start(s32[1,5]{1,0:T(1,128)} %pattern_ref.1) | copy-start | bytes 64
where the time goes:
time: 46.3 us; the launch traced here: 45.7 us
  Pallas kernels  39.8 us (86%)
  local copies, waits for them, and re-layouts  5.26 us (11%)
  between operations  0.65 us (1%)
    pallas_call x1, Pallas kernels, on_device(): pl.pallas_call(functools.partial(kernel, owners, shares), out_shape=jax.S...  39.8 us
    unnamed x14, local copies, waits for them, and re-layouts  3.36 us

commit v1 on v0

--- a/solution.py
+++ b/solution.py
@@ -208,6 +208,16 @@
     pattern_ref,
     prior_ref,
     out_ref,
+    block_in,
+    hits_in,
+    slot_in,
+    kept_in,
+    derivs_in,
+    resid_in,
+    invsig_in,
+    pattern_in,
+    prior_in,
+    input_sem,
     onehot,
     table,
     part,
@@ -226,6 +236,18 @@
     blk, trk = lax.axis_index("blk"), lax.axis_index("trk")
     rows = block_ref.shape[1]
     tracks = kept_ref.shape[1]
+    outside = (
+        pattern_ref, kept_ref, invsig_ref, derivs_ref, resid_ref, block_ref, hits_ref, slot_ref, prior_ref
+    )
+    inside = (
+        pattern_in, kept_in, invsig_in, derivs_in, resid_in, block_in, hits_in, slot_in, prior_in
+    )
+    fetches = [
+        pltpu.make_async_copy(source, target, input_sem.at[i])
+        for i, (source, target) in enumerate(zip(outside, inside))
+    ]
+    for one in fetches:
+        one.start()
     modules = owners * MODS
     order_size = MODS * PAR
     per_share = LANES // MODS
@@ -233,10 +255,16 @@
     def other_blk(distance):
         return {"blk": lax.rem(blk + distance, owners), "trk": trk}
 
-    def other_trk(distance):
-        return {"blk": blk, "trk": lax.rem(trk + distance, shares)}
-
-    peers = [other_blk(d) for d in range(1, owners)] + [other_trk(d) for d in range(1, shares)]
+    pairs, width = shares // 2, shares // 2
+    pair, half = trk // 2, lax.rem(trk, 2)
+    sibling = {"blk": blk, "trk": pair * 2 + 1 - half}
+
+    def other_pair(c, j):
+        return {"blk": lax.rem(blk + c, owners), "trk": lax.rem(pair + j, pairs) * 2 + half}
+
+    steps = [(c, j) for c in range(owners) for j in range(pairs) if c or j]
+    steps.sort(key=lambda step: (abs(step[0] - owners // 2), -step[1]))
+    peers = [sibling] + [other_pair(c, j) for c, j in steps]
     barrier = pltpu.get_barrier_semaphore()
     for peer in peers:
         pl.semaphore_signal(barrier, inc=1, device_id=peer, device_id_type=pl.DeviceIdType.MESH)
@@ -252,8 +280,9 @@
         )
 
     started = []
-
-    table[blk, :, 0:NB] = pattern_ref[...]
+    fetches[0].wait()
+
+    table[blk, :, 0:NB] = pattern_in[...]
     pl.semaphore_wait(barrier, len(peers))
     sent = [
         copy(table.at[blk], table.at[blk], table_send.at[d - 1], table_recv.at[d - 1], other_blk(d))
@@ -263,16 +292,19 @@
         one.start()
     started += sent
 
+    for one in fetches[1:]:
+        one.wait()
+
     track_of = lax.broadcasted_iota(jnp.int32, (tracks, rows), 1) // SEG
     track_id = lax.broadcasted_iota(jnp.int32, (tracks, rows), 0)
     kept_rows = jnp.dot(
-        jnp.broadcast_to(kept_ref[...].astype(jnp.float32), (WIDE, tracks)).astype(jnp.bfloat16),
+        jnp.broadcast_to(kept_in[...].astype(jnp.float32), (WIDE, tracks)).astype(jnp.bfloat16),
         (track_of == track_id).astype(jnp.float32).astype(jnp.bfloat16),
         preferred_element_type=jnp.float32,
     )[0:1]
-    scaling = kept_rows * invsig_ref[...].astype(jnp.float32)
-    scaled = (scaling * derivs_ref[...].astype(jnp.float32)).astype(jnp.bfloat16).astype(jnp.float32)
-    weighted = (scaling * resid_ref[...].astype(jnp.float32)).astype(jnp.bfloat16).astype(jnp.float32)
+    scaling = kept_rows * invsig_in[...].reshape(1, rows).astype(jnp.float32)
+    scaled = (scaling * derivs_in[...].astype(jnp.float32)).astype(jnp.bfloat16).astype(jnp.float32)
+    weighted = (scaling * resid_in[...].reshape(1, rows).astype(jnp.float32)).astype(jnp.bfloat16).astype(jnp.float32)
     none = jnp.zeros((WIDE - PAR, rows), jnp.float32)
     derivs = jnp.concatenate(
         [
@@ -281,27 +313,30 @@
         ],
         axis=1,
     )
-    first_block = block_ref[...]
-    first_module = first_block * MODS + hits_ref[0:1]
+    first_block = block_in[...]
+    first_module = first_block * MODS + hits_in[0:1]
     module_ids = lax.broadcasted_iota(jnp.int32, (modules, rows), 0)
     onehot[:, 0:rows] = (module_ids == first_module).astype(jnp.float32).astype(jnp.bfloat16)
 
     place_row = lax.broadcasted_iota(jnp.int32, (order_size, LANES), 0) // PAR
     place_lane = lax.broadcasted_iota(jnp.int32, (order_size, LANES), 1)
-    half = lax.rem(blk, per_share)
-    place = (place_lane == place_row + half * MODS).astype(jnp.float32).astype(jnp.bfloat16)
+    lane_half = lax.rem(blk, per_share)
+    place = (place_lane == place_row + lane_half * MODS).astype(jnp.float32).astype(jnp.bfloat16)
     component = lax.broadcasted_iota(jnp.int32, (WIDE, order_size), 0)
     parameter = lax.broadcasted_iota(jnp.int32, (WIDE, order_size), 1)
     own_entry = component == lax.rem(parameter, PAR)
-    spread_prior = jnp.where(own_entry, prior_ref[...], 0.0)
+    spread_prior = jnp.where(own_entry, prior_in[...], 0.0)
     prior_parts = jnp.dot(three_parts(spread_prior), place, preferred_element_type=jnp.float32)
     own_prior = prior_parts[0:WIDE] + prior_parts[WIDE : 2 * WIDE] + prior_parts[2 * WIDE :]
     own_prior = jnp.where(trk == 0, own_prior, 0.0)
     own_share = blk // per_share
     prior = [jnp.where(own_share == j, own_prior, 0.0) for j in range(shares)]
 
-    def in_order(vector_ref):
-        parts = three_parts(vector_ref[own_share])
+    def in_order(vector):
+        own = jnp.zeros((WIDE, LANES), jnp.float32)
+        for j in range(shares):
+            own = jnp.where(own_share == j, vector[:, j * LANES : (j + 1) * LANES], own)
+        parts = three_parts(own)
         laid = lax.dot_general(
             parts, place, (((1,), (1,)), ((), ())), preferred_element_type=jnp.float32
         )
@@ -313,12 +348,12 @@
     patterns = table[...].reshape(owners, LANES).astype(jnp.float32)
     block_ids = lax.broadcasted_iota(jnp.int32, (owners, rows), 0)
     names = (block_ids == first_block).astype(jnp.float32)
-    slot = slot_ref[...]
+    slot = slot_in[...]
     second_block = jnp.zeros((1, rows), jnp.float32)
     for s in range(NB):
         value = jnp.sum(names * patterns[:, s : s + 1], axis=0, keepdims=True)
         second_block = jnp.where(slot == s, value, second_block)
-    second_module = second_block.astype(jnp.int32) * MODS + hits_ref[1:2]
+    second_module = second_block.astype(jnp.int32) * MODS + hits_in[1:2]
     onehot[:, rows : 2 * rows] = (module_ids == second_module).astype(jnp.float32).astype(jnp.bfloat16)
 
     def scatter(row_values):
@@ -339,64 +374,49 @@
 
     def add_up(phase, terms):
         for j in range(shares):
-            part[phase, j] = terms[j]
-        sent = []
-        for d in range(1, shares):
-            sent.append(
-                copy(
-                    part.at[phase, lax.rem(trk + d, shares)],
-                    landed.at[phase, d - 1],
-                    part_send.at[phase, d - 1],
-                    part_recv.at[phase, d - 1],
-                    other_trk(d),
-                )
+            part[phase, j // width, j % width] = terms[j]
+        swap = copy(
+            part.at[phase, 1 - half, :, 0:PAR],
+            landed.at[phase, :, 0:PAR],
+            part_send.at[phase],
+            part_recv.at[phase],
+            sibling,
+        )
+        swap.start()
+        own = part[phase, half]
+        swap.wait_recv()
+        blocks[phase, blk, pair] = own + landed[phase]
+        sent = [
+            copy(
+                blocks.at[phase, blk, pair, :, 0:PAR],
+                blocks.at[phase, blk, pair, :, 0:PAR],
+                block_send.at[phase, c, j],
+                block_recv.at[phase, c, j],
+                other_pair(c, j),
             )
-        for one in sent:
-            one.start()
-        own = part[phase, trk]
-        for one in sent:
-            one.wait_recv()
-        started.extend(sent)
-        for d in range(1, shares):
-            own = own + landed[phase, d - 1]
-        blocks[phase, blk] = own
-        sent = []
-        for d in range(1, owners):
-            sent.append(
-                copy(
-                    blocks.at[phase, blk],
-                    blocks.at[phase, blk],
-                    block_send.at[phase, d - 1],
-                    block_recv.at[phase, d - 1],
-                    other_blk(d),
-                )
-            )
+            for c, j in steps
+        ]
         for one in sent:
             one.start()
         for one in sent:
             one.wait_recv()
-        started.extend(sent)
-        summed = blocks[phase, 0]
-        for k in range(1, owners):
-            summed = summed + blocks[phase, k]
-        full[phase, trk] = summed
-        sent = []
-        for d in range(1, shares):
-            sent.append(
-                copy(
-                    full.at[phase, trk],
-                    full.at[phase, trk],
-                    full_send.at[phase, d - 1],
-                    full_recv.at[phase, d - 1],
-                    other_trk(d),
-                )
-            )
-        for one in sent:
-            one.start()
-        for one in sent:
-            one.wait_recv()
-        started.extend(sent)
-        return jnp.concatenate([full[phase, j] for j in range(shares)], axis=1)
+        summed = blocks[phase, 0, 0, :, 0:PAR]
+        for k in range(1, owners * pairs):
+            summed = summed + blocks[phase, k // pairs, k % pairs, :, 0:PAR]
+        full[phase, half, :, 0:PAR] = summed
+        join = copy(
+            full.at[phase, half, :, 0:PAR],
+            full.at[phase, half, :, 0:PAR],
+            full_send.at[phase],
+            full_recv.at[phase],
+            sibling,
+        )
+        join.start()
+        join.wait_recv()
+        started.extend([swap, join] + sent)
+        read = [full[phase, j // width, j % width, 0:PAR] for j in range(shares)]
+        empty = jnp.zeros((WIDE - PAR, shares * LANES), jnp.float32)
+        return jnp.concatenate([jnp.concatenate(read, axis=1), empty], axis=0)
 
     def pieces(vector):
         return [vector[:, j * LANES : (j + 1) * LANES] for j in range(shares)]
@@ -419,7 +439,7 @@
         off_terms.append(beta_next)
         basis_list.append(current)
         previous, current, beta_term = (current, direction / beta_next, beta_next)
-    out_ref[1:2] = in_order(full.at[0])
+    out_ref[1:2] = in_order(gradient)
 
     first, second = diag_terms
     below, last = off_terms
@@ -434,9 +454,7 @@
     back_next = forward_next / tip
     back = (forward - lower * back_next) / root
     result = back * basis_list[0] + back_next * basis_list[1]
-    for j, values in enumerate(pieces(result)):
-        part[PHASES, j] = values
-    out_ref[0:1] = in_order(part.at[PHASES])
+    out_ref[0:1] = in_order(result)
     for one in started:
         one.wait_send()
 
@@ -457,34 +475,45 @@
     args = (
         row_block, row_hits, row_slot, track_kept, row_derivs, row_resid, row_invsig, pattern, prior
     )
-    if owners * MODS != shares * LANES:
+    if owners * MODS != shares * LANES or shares % 2:
         return on_device_large(*args)
     rows = row_resid.shape[0]
     dma = pltpu.SemaphoreType.DMA
     tile = (WIDE, LANES)
+    width = shares // 2
     out = pl.pallas_call(
         functools.partial(kernel, owners, shares),
         out_shape=jax.ShapeDtypeStruct((2, MODS * PAR), jnp.float32),
-        in_specs=[pl.BlockSpec(memory_space=pltpu.VMEM)] * 9,
+        in_specs=[pl.BlockSpec(memory_space=pltpu.HBM)] * 9,
         out_specs=pl.BlockSpec(memory_space=pltpu.VMEM),
         scratch_shapes=[
+            pltpu.VMEM((1, rows), jnp.int32),
+            pltpu.VMEM((2, rows), jnp.int32),
+            pltpu.VMEM((1, rows), jnp.int32),
+            pltpu.VMEM((1, track_kept.shape[0]), jnp.int32),
+            pltpu.VMEM((2 * PAR, rows), jnp.bfloat16),
+            pltpu.VMEM((rows,), jnp.bfloat16),
+            pltpu.VMEM((rows,), jnp.bfloat16),
+            pltpu.VMEM((1, NB), jnp.int32),
+            pltpu.VMEM((1, MODS * PAR), jnp.float32),
+            dma((9,)),
             pltpu.VMEM((owners * MODS, 2 * rows), jnp.bfloat16),
             pltpu.VMEM((owners, 1, LANES), jnp.int32),
-            pltpu.VMEM((PHASES + 1, shares) + tile, jnp.float32),
-            pltpu.VMEM((PHASES, shares - 1) + tile, jnp.float32),
-            pltpu.VMEM((PHASES, owners) + tile, jnp.float32),
-            pltpu.VMEM((PHASES + 1, shares) + tile, jnp.float32),
+            pltpu.VMEM((PHASES, 2, width) + tile, jnp.float32),
+            pltpu.VMEM((PHASES, width) + tile, jnp.float32),
+            pltpu.VMEM((PHASES, owners, shares // 2, width) + tile, jnp.float32),
+            pltpu.VMEM((PHASES, 2, width) + tile, jnp.float32),
             dma((owners - 1,)),
             dma((owners - 1,)),
-            dma((PHASES, shares - 1)),
-            dma((PHASES, shares - 1)),
-            dma((PHASES, owners - 1)),
-            dma((PHASES, owners - 1)),
-            dma((PHASES, shares - 1)),
-            dma((PHASES, shares - 1)),
+            dma((PHASES,)),
+            dma((PHASES,)),
+            dma((PHASES, owners, shares // 2)),
+            dma((PHASES, owners, shares // 2)),
+            dma((PHASES,)),
+            dma((PHASES,)),
         ],
         compiler_params=pltpu.CompilerParams(
-            collective_id=0, has_side_effects=True, vmem_limit_bytes=16 * 1024 * 1024
+            collective_id=0, has_side_effects=True, vmem_limit_bytes=60 * 1024 * 1024
         ),
     )(
         row_block.reshape(1, rows),
@@ -492,8 +521,8 @@
         row_slot.reshape(1, rows),
         track_kept.reshape(1, -1),
         row_derivs,
-        row_resid.reshape(1, rows),
-        row_invsig.reshape(1, rows),
+        row_resid,
+        row_invsig,
         pattern,
         prior,
     )

time: 46.3 us -> 36.7 us (0.79)
  Pallas kernels: 39.8 us -> 34.5 us
  local copies, waits for them, and re-layouts: 5.26 us -> 1.32 us
    pallas_call x1, Pallas kernels: 39.8 us -> 34.5 us  [on_device(): pl.pallas_call(functools.partial(kernel, owners, shares), out_shape=jax.S...]
    unnamed x14 -> x0, local copies, waits for them, and re-layouts: 3.36 us -> none
    reshape x2 -> x0, local copies, waits for them, and re-layouts: 1.34 us -> none  [the longest x1 0.67 us: on_device(): row_invsig.reshape(1, rows)]
    slice x1, local copies, waits for them, and re-layouts: 0.57 us -> 1.32 us  [on_device(): return (out[0:1], out[1:2])]
where the time goes in v1:
time: 36.7 us; the launch traced here: 36.5 us
  Pallas kernels  34.5 us (94%)
  local copies, waits for them, and re-layouts  1.32 us (4%)
  between operations  0.64 us (2%)
    pallas_call x1, Pallas kernels, on_device(): pl.pallas_call(functools.partial(kernel, owners, shares), out_shape=jax.S...  34.5 us
    slice x1, local copies, waits for them, and re-layouts, on_device(): return (out[0:1], out[1:2])  1.32 us

profile of v1, /device:TPU:1, one launch (start us, length us, event | category | flops | bytes accessed | tf_op | source)
XLA Modules:
  0.0 36.5 jit_solution(17852012321872814622)
XLA Ops:
  0.6 34.5 %shard_map.104 = f32[2,384]{1,0:T(2,128)} custom-call(s32[1,256]{1,0:T(1,128)} %bitcast.3, s32[2,256]{1,0:T(2,128)} %hits_ref.1, s32[1,256]{1,0:T(1,128)} %bitcast.4, s32[1,32]{1,0:T(1,128)} %bitcast.5, bf16[12,256]{1,0:T(8,128)(2,1)} %derivs_ref.1, bf16[256]{0:T(256)(128)(2,1)} %resid_ref.1, bf16[256]{0:T(256)(128)(2,1)} %invsig_ref.1, s32[1,5]{1,0:T(1,128)} %pattern_ref.1, ...), custom_call_target="tpu_custom_call" | custom-call | tf_op jit(solution)/shard_map/pallas_call | solution.py:484
  35.2 1.3 %fusion = (f32[1,384]{1,0:T(1,128)}, f32[1,384]{1,0:T(1,128)}) fusion(f32[2,384]{1,0:T(2,128)} %shard_map.104), kind=kLoop, calls=%fused_computation | loop fusion | bytes 6144 | tf_op jit(solution)/shard_map/slice | solution.py:529

commit v2 on v1

--- a/solution.py
+++ b/solution.py
@@ -372,7 +372,7 @@
         along = jnp.sum(derivs * read, axis=0, keepdims=True)
         return along[:, 0:rows] + along[:, rows : 2 * rows]
 
-    def add_up(phase, terms):
+    def add_up(phase, terms, beside=None):
         for j in range(shares):
             part[phase, j // width, j % width] = terms[j]
         swap = copy(
@@ -398,6 +398,8 @@
         ]
         for one in sent:
             one.start()
+        if beside is not None:
+            beside()
         for one in sent:
             one.wait_recv()
         summed = blocks[phase, 0, 0, :, 0:PAR]
@@ -427,11 +429,15 @@
     previous = jnp.zeros_like(gradient)
     beta_term = jnp.zeros((1, 1), jnp.float32)
     diag_terms, off_terms, basis_list = ([], [], [])
+
+    def lay_gradient():
+        out_ref[1:2] = in_order(gradient)
+
     for iteration in range(ITERS):
         terms = pieces(scatter(gather(current)))
         for j, values in enumerate(pieces(current)):
             terms[j] = terms[j] + prior[j] * values
-        image_vec = add_up(iteration + 1, terms)
+        image_vec = add_up(iteration + 1, terms, None if iteration else lay_gradient)
         alpha_term = total(current * image_vec)
         direction = image_vec - alpha_term * current - beta_term * previous
         beta_next = jnp.sqrt(total(direction * direction) + epsilon)
@@ -439,7 +445,6 @@
         off_terms.append(beta_next)
         basis_list.append(current)
         previous, current, beta_term = (current, direction / beta_next, beta_next)
-    out_ref[1:2] = in_order(gradient)
 
     first, second = diag_terms
     below, last = off_terms

time: 36.7 us -> 36.7 us (level)
  no operation moved by 1% of the time
where the time goes in v2:
time: 36.7 us; the launch traced here: 36.5 us
  Pallas kernels  34.5 us (94%)
  local copies, waits for them, and re-layouts  1.32 us (4%)
  between operations  0.64 us (2%)
    pallas_call x1, Pallas kernels, on_device(): pl.pallas_call(functools.partial(kernel, owners, shares), out_shape=jax.S...  34.5 us
    slice x1, local copies, waits for them, and re-layouts, on_device(): return (out[0:1], out[1:2])  1.32 us

profile of v2, /device:TPU:1, one launch (start us, length us, event | category | flops | bytes accessed | tf_op | source)
XLA Modules:
  0.0 36.5 jit_solution(7815453184094426676)
XLA Ops:
  0.6 34.5 %shard_map.104 = f32[2,384]{1,0:T(2,128)} custom-call(s32[1,256]{1,0:T(1,128)} %bitcast.3, s32[2,256]{1,0:T(2,128)} %hits_ref.1, s32[1,256]{1,0:T(1,128)} %bitcast.4, s32[1,32]{1,0:T(1,128)} %bitcast.5, bf16[12,256]{1,0:T(8,128)(2,1)} %derivs_ref.1, bf16[256]{0:T(256)(128)(2,1)} %resid_ref.1, bf16[256]{0:T(256)(128)(2,1)} %invsig_ref.1, s32[1,5]{1,0:T(1,128)} %pattern_ref.1, ...), custom_call_target="tpu_custom_call" | custom-call | tf_op jit(solution)/shard_map/pallas_call | solution.py:489
  35.2 1.3 %fusion = (f32[1,384]{1,0:T(1,128)}, f32[1,384]{1,0:T(1,128)}) fusion(f32[2,384]{1,0:T(2,128)} %shard_map.104), kind=kLoop, calls=%fused_computation | loop fusion | bytes 6144 | tf_op jit(solution)/shard_map/slice | solution.py:534
